TPU v7x, 32 devices: a whole 2x2x4 slice. The times are simulated.
32 devices in a mesh: dp: 2 (over x), expert: 16 (over z, y, core).
Axes of the slice: x: 2, y: 2, z: 4, core: 2. Of those that a mesh axis runs over, the one named last changes fastest.
Arguments:
- tokens: bfloat16 [128, 4096], P(('dp', 'expert')), may hold values from -6 to 6
- grad_output: bfloat16 [128, 4096], P(('dp', 'expert')), may hold values from -6 to 6
- routes: int32 [128, 8], P(('dp', 'expert')), may hold values from 0 to 15, all different within a row; in each aligned block of 4 rows (0 to 3, 4 to 7, ...) at most 3 rows name the same one
- gate_weights: float32 [128, 8], P(('dp', 'expert')), may hold values from 0.05 to 1
- gate_proj: bfloat16 [16, 1536, 4096], P('expert', 'dp'), may hold values from -0.09375 to 0.09375
- up_proj: bfloat16 [16, 1536, 4096], P('expert', 'dp'), may hold values from -0.09375 to 0.09375
- down_proj: bfloat16 [16, 1536, 4096], P('expert', 'dp'), may hold values from -0.15625 to 0.15625
Outputs:
- layer_out: bfloat16 [128, 4096], P(('dp', 'expert'))
- grad_tokens: bfloat16 [128, 4096], P(('dp', 'expert'))
- grad_gates: float32 [128, 8], P(('dp', 'expert'))
- grad_gate_proj: bfloat16 [16, 1536, 4096], P('expert', 'dp')
- grad_up_proj: bfloat16 [16, 1536, 4096], P('expert', 'dp')
- grad_down_proj: bfloat16 [16, 1536, 4096], P('expert', 'dp')
Inputs may be any that keep to these rules, and one draw needn't show every extreme that they name: `routes`: each row names 8 different experts. Among the 4 tokens of one device no expert is named by more than 3 tokens, a bound that some block reaches.
All inputs are finite; a program needn't handle non-finite values.
Results may differ from a plain program's by a relative error of at most 0.0095.
Values may be sent and summed in bfloat16 or wider, within the bound.
A program may use at most 128 MiB of HBM per device.

v0:
```python
import jax
import jax.numpy as jnp
from jax import lax
from jax.sharding import PartitionSpec as P


def silu_parts(pre_act):
    squash = jax.nn.sigmoid(pre_act)
    return (pre_act * squash, squash * (1.0 + pre_act * (1.0 - squash)))


def contract_last(left, right):
    return lax.dot_general(
        left, right, (((1,), (1,)), ((), ())), preferred_element_type=jnp.float32
    )


def contract_first(left, right):
    return lax.dot_general(
        left, right, (((0,), (0,)), ((), ())), preferred_element_type=jnp.float32
    )


def exact_dot(left, right):
    return jnp.dot(left, right, precision=lax.Precision.HIGHEST)


def expert_rows(x_rows, g_rows, gate_part, up_part, down_part):
    pre_gate = contract_last(x_rows, gate_part)
    pre_up = contract_last(x_rows, up_part)
    active, slope_term = silu_parts(pre_gate)
    hidden = (active * pre_up).astype(jnp.bfloat16)
    out_part = jnp.dot(hidden, down_part, preferred_element_type=jnp.float32).astype(jnp.bfloat16)
    d_hidden = contract_last(g_rows, down_part)
    d_upper = (d_hidden * active).astype(jnp.bfloat16)
    d_lower = (d_hidden * pre_up * slope_term).astype(jnp.bfloat16)
    back_part = (
        jnp.dot(d_lower, gate_part, preferred_element_type=jnp.float32)
        + jnp.dot(d_upper, up_part, preferred_element_type=jnp.float32)
    ).astype(jnp.bfloat16)
    grad_list = (
        contract_first(d_lower, x_rows),
        contract_first(d_upper, x_rows),
        contract_first(hidden, g_rows),
    )
    return (out_part, back_part, grad_list)


def make_slots(routes, experts, slot_cap):
    flat_ids = routes.reshape(-1)
    expert_ids = jnp.arange(experts, dtype=jnp.int32)
    onehot = (flat_ids[:, None] == expert_ids[None, :]).astype(jnp.int32)
    earlier = jnp.sum((jnp.cumsum(onehot, axis=0) - onehot) * onehot, axis=1)
    slot_index = flat_ids * slot_cap + earlier
    positions = jnp.arange(experts * slot_cap, dtype=jnp.int32)
    return (slot_index[:, None] == positions[None, :]).astype(jnp.float32)


def dispatch(tokens, grad_output, routes, gate_weights, experts, slot_cap):
    token_count, top_count = routes.shape
    slot_table = make_slots(routes, experts, slot_cap)
    by_token = jnp.sum(slot_table.reshape(token_count, top_count, -1), axis=1)
    picker = by_token.astype(jnp.bfloat16)
    x_slots = contract_first(picker, tokens).astype(jnp.bfloat16)
    dy_slots = contract_first(picker, grad_output)
    slot_gate = lax.dot_general(
        slot_table,
        gate_weights.reshape(-1),
        (((0,), (0,)), ((), ())),
        precision=lax.Precision.HIGHEST,
    )
    g_slots = (slot_gate[:, None] * dy_slots).astype(jnp.bfloat16)
    return (slot_table, by_token, dy_slots, x_slots, g_slots)


def combine(slot_table, by_token, dy_slots, gate_weights, out_rows, back_rows):
    token_count, top_count = gate_weights.shape
    weighted = jnp.sum(
        slot_table.reshape(token_count, top_count, -1) * gate_weights[:, :, None], axis=1
    )
    layer_out = exact_dot(weighted, out_rows)
    grad_tokens = exact_dot(by_token, back_rows)
    inner_prods = jnp.sum(dy_slots * out_rows, axis=1)
    grad_gates = exact_dot(slot_table, inner_prods).reshape(token_count, top_count)
    return (layer_out, grad_tokens, grad_gates)


def body(tokens, grad_output, routes, gate_weights, gate_proj, up_proj, down_proj):
    experts = lax.axis_size("expert")
    groups = lax.axis_size("dp")
    token_count, top_count = routes.shape
    feature_dim = tokens.shape[1]
    slot_cap = min(
        token_count, max(2, (3 * token_count * top_count + 2 * experts - 1) // (2 * experts))
    )
    gate_local = gate_proj[0]
    up_local = up_proj[0]
    down_local = down_proj[0]
    group_x, group_dy = (
        lax.all_gather(tokens, "dp", axis=0, tiled=True),
        lax.all_gather(grad_output, "dp", axis=0, tiled=True),
    )
    group_routes = lax.all_gather(routes, "dp", axis=0, tiled=True)
    group_gate = lax.all_gather(gate_weights, "dp", axis=0, tiled=True)
    group_cap = slot_cap * groups
    slot_table, by_token, dy_slots, x_slots, g_slots = dispatch(
        group_x, group_dy, group_routes, group_gate, experts, group_cap
    )
    x_in, g_in = (
        lax.all_to_all(
            x_slots.reshape(experts, group_cap, feature_dim),
            "expert",
            split_axis=0,
            concat_axis=0,
            tiled=True,
        ),
        lax.all_to_all(
            g_slots.reshape(experts, group_cap, feature_dim),
            "expert",
            split_axis=0,
            concat_axis=0,
            tiled=True,
        ),
    )
    out_part, back_part, grad_list = expert_rows(
        x_in.reshape(-1, feature_dim),
        g_in.reshape(-1, feature_dim),
        gate_local,
        up_local,
        down_local,
    )
    out_home, back_home = (
        lax.all_to_all(
            out_part.reshape(experts, group_cap, feature_dim),
            "expert",
            split_axis=0,
            concat_axis=0,
            tiled=True,
        ),
        lax.all_to_all(
            back_part.reshape(experts, group_cap, feature_dim),
            "expert",
            split_axis=0,
            concat_axis=0,
            tiled=True,
        ),
    )
    part_out, part_back, part_gates = combine(
        slot_table,
        by_token,
        dy_slots,
        group_gate,
        out_home.reshape(-1, feature_dim).astype(jnp.float32),
        back_home.reshape(-1, feature_dim).astype(jnp.float32),
    )
    layer_out, grad_tokens, grad_gates = (
        lax.psum_scatter(
            part_out.astype(jnp.bfloat16), "dp", scatter_dimension=0, tiled=True
        ).astype(jnp.float32),
        lax.psum_scatter(
            part_back.astype(jnp.bfloat16), "dp", scatter_dimension=0, tiled=True
        ).astype(jnp.float32),
        lax.psum_scatter(
            part_gates.astype(jnp.bfloat16), "dp", scatter_dimension=0, tiled=True
        ).astype(jnp.float32),
    )
    return (
        layer_out.astype(jnp.bfloat16),
        grad_tokens.astype(jnp.bfloat16),
        grad_gates,
        grad_list[0].astype(jnp.bfloat16)[None],
        grad_list[1].astype(jnp.bfloat16)[None],
        grad_list[2].astype(jnp.bfloat16)[None],
    )


def solution(mesh):
    in_specs = (
        P(("dp", "expert"), None),
        P(("dp", "expert"), None),
        P(("dp", "expert"), None),
        P(("dp", "expert"), None),
        P("expert", "dp", None),
        P("expert", "dp", None),
        P("expert", "dp", None),
    )
    out_specs = (
        P(("dp", "expert"), None),
        P(("dp", "expert"), None),
        P(("dp", "expert"), None),
        P("expert", "dp", None),
        P("expert", "dp", None),
        P("expert", "dp", None),
    )
    return jax.shard_map(body, mesh=mesh, in_specs=in_specs, out_specs=out_specs, check_vma=False)
```

profile of v0, /device:TPU:0, one launch (start us, length us, event | category | flops | bytes accessed | tf_op | source)
XLA Modules:
  0.0 205.2 jit_solution(10613584228352960687)
XLA Ops:
  7.2 5.4 %all-gather = s32[2,4,8]{2,1,0:T(4,128)S(1)} all-gather(s32[1,4,8]{2,1,0:T(4,128)} %bitcast.75), channel_id=1, replica_groups=mesh['dp'=2,'expert'=16] {'dp'}, dimensions={0}, use_global_device_ids=true | all-gather | bytes 384 | tf_op jit(solution)/shard_map/all_gather | solution.py:103
  12.7 4.5 %all-gather.1 = f32[2,4,8]{2,1,0:T(4,128)S(1)} all-gather(f32[1,4,8]{2,1,0:T(4,128)} %bitcast.76), channel_id=1, replica_groups=mesh['dp'=2,'expert'=16] {'dp'}, dimensions={0}, use_global_device_ids=true | all-gather | bytes 384 | tf_op jit(solution)/shard_map/all_gather | solution.py:104
  17.6 4.8 %all-gather.2 = bf16[2,4,4096]{2,1,0:T(4,128)(2,1)S(1)} all-gather(bf16[1,4,4096]{2,1,0:T(4,128)(2,1)} %bitcast.71), channel_id=1, replica_groups=mesh['dp'=2,'expert'=16] {'dp'}, dimensions={0}, use_global_device_ids=true | all-gather | bytes 98304 | tf_op jit(solution)/shard_map/all_gather | solution.py:100
  23.8 31.1 %all_to_all.20 = bf16[16,6,4096]{2,1,0:T(8,128)(2,1)S(1)} all-to-all(bf16[16,6,4096]{2,1,0:T(8,128)(2,1)S(1)} %reshape.72), channel_id=1, replica_groups=mesh['dp'=2,'expert'=16] {'expert'}, dimensions={0} | all-to-all | bytes 1572864 | tf_op jit(solution)/shard_map/all_to_all | solution.py:110
  55.2 5.0 %fusion.10 = f32[96,768]{1,0:T(8,128)S(1)} fusion(bf16[96,4096]{1,0:T(8,128)(2,1)S(1)} %reshape.73, bf16[1,768,4096]{2,1,0:T(8,128)(2,1)} %param.11), kind=kOutput, calls=%fused_computation.13 | convolution fusion | flops 603979776 | bytes 7372800 | tf_op jit(solution)/shard_map/dot_general | solution.py:13
  60.2 5.7 %multiply_convert_fusion.3 = (bf16[96,768]{1,0:T(8,128)(2,1)S(1)}, f32[96,768]{1,0:T(8,128)}) fusion(f32[96,768]{1,0:T(8,128)S(1)} %fusion.10, bf16[96,4096]{1,0:T(8,128)(2,1)S(1)} %reshape.73, bf16[1,768,4096]{2,1,0:T(8,128)(2,1)} %param.12), kind=kOutput, calls=%fused_computation.29 | convolution fusion | flops 604422144 | bytes 7815168 | tf_op jit(solution)/shard_map/dot_general | solution.py:13
  67.1 1.2 reshape.74
  68.3 5.0 %all-to-all-start.1 = ((bf16[16,6,4096]{2,1,0:T(8,128)(2,1)}), bf16[16,6,4096]{2,1,0:T(8,128)(2,1)S(1)}, u32[]{:S(2)}, u32[]{:S(2)}) async-start(bf16[16,6,4096]{2,1,0:T(8,128)(2,1)} %reshape.74), calls=%async_computation.1 | async-start | bytes 2097152 | tf_op jit(solution)/shard_map/all_to_all | solution.py:133
  73.4 4.6 %all-gather.3 = bf16[2,4,4096]{2,1,0:T(4,128)(2,1)S(1)} all-gather(bf16[1,4,4096]{2,1,0:T(4,128)(2,1)S(1)} %bitcast.72), channel_id=1, replica_groups=mesh['dp'=2,'expert'=16] {'dp'}, dimensions={0}, use_global_device_ids=true | all-gather | bytes 98304 | tf_op jit(solution)/shard_map/all_gather | solution.py:101
  78.2 18.0 %all-to-all-done.1 = bf16[16,6,4096]{2,1,0:T(8,128)(2,1)S(1)} async-done(((bf16[16,6,4096]{2,1,0:T(8,128)(2,1)}), bf16[16,6,4096]{2,1,0:T(8,128)(2,1)S(1)}, u32[]{:S(2)}, u32[]{:S(2)}) %all-to-all-start.1) | async-done | bytes 786464 | tf_op jit(solution)/shard_map/all_to_all | solution.py:133
  98.8 31.9 %all_to_all.21 = bf16[16,6,4096]{2,1,0:T(8,128)(2,1)} all-to-all(bf16[16,6,4096]{2,1,0:T(8,128)(2,1)} %reshape.77), channel_id=1, replica_groups=mesh['dp'=2,'expert'=16] {'expert'}, dimensions={0} | all-to-all | bytes 1572864 | tf_op jit(solution)/shard_map/all_to_all | solution.py:117
  130.8 2.2 %reshape.78 = bf16[96,4096]{1,0:T(8,128)(2,1)} reshape(bf16[16,6,4096]{2,1,0:T(8,128)(2,1)} %all_to_all.21) | data formatting | bytes 1572864 | tf_op jit(solution)/shard_map/reshape | solution.py:127
  133.0 5.2 %multiply_convert_fusion.2 = (bf16[96,768]{1,0:T(8,128)(2,1)S(1)}, bf16[96,768]{1,0:T(8,128)(2,1)S(1)}) fusion(f32[96,768]{1,0:T(8,128)S(1)} %fusion.10, f32[96,768]{1,0:T(8,128)} %get-tuple-element.15, bf16[96,4096]{1,0:T(8,128)(2,1)} %reshape.78, bf16[1,768,4096]{2,1,0:T(8,128)(2,1)} %param.13), kind=kOutput, calls=%fused_computation.28 | convolution fusion | flops 604938240 | bytes 7962624 | tf_op jit(solution)/shard_map/dot_general | solution.py:13
  143.6 5.0 %all-to-all-start.3 = ((bf16[16,6,4096]{2,1,0:T(8,128)(2,1)}), bf16[16,6,4096]{2,1,0:T(8,128)(2,1)S(1)}, u32[]{:S(2)}, u32[]{:S(2)}) async-start(bf16[16,6,4096]{2,1,0:T(8,128)(2,1)} %reshape.79), calls=%async_computation.3 | async-start | bytes 2097152 | tf_op jit(solution)/shard_map/all_to_all | solution.py:140
  148.7 1.3 dynamic-slice
  152.2 5.6 %all-reduce.2 = bf16[8,8]{1,0:T(8,128)(2,1)} all-reduce(bf16[8,8]{1,0:T(8,128)(2,1)} %convert_element_type.73), channel_id=4, replica_groups=mesh['dp'=2,'expert'=16] {'dp'}, use_global_device_ids=true, to_apply=%region_7.8.clone | all-reduce | flops 64 | bytes 256
  157.8 1.3 dynamic-slice_convert_fusion
  159.1 1.7 convolution_convert_fusion.5
  160.9 4.5 %fusion.14 = bf16[1,768,4096]{2,1,0:T(8,128)(2,1)} fusion(bf16[96,768]{1,0:T(8,128)(2,1)S(1)} %get-tuple-element.14, bf16[96,4096]{1,0:T(8,128)(2,1)S(1)} %copy-done.2), kind=kOutput, calls=%fused_computation.17 | convolution fusion | flops 607125504 | bytes 7225344 | tf_op jit(solution)/shard_map/dot_general | solution.py:19
  165.4 4.5 %fusion.12 = bf16[1,768,4096]{2,1,0:T(8,128)(2,1)} fusion(bf16[96,768]{1,0:T(8,128)(2,1)S(1)} %copy-done.6, bf16[96,4096]{1,0:T(8,128)(2,1)S(1)} %reshape.73), kind=kOutput, calls=%fused_computation.15 | convolution fusion | flops 607125504 | bytes 7225344 | tf_op jit(solution)/shard_map/dot_general | solution.py:19
  169.9 1.6 all-to-all-done.3
  172.9 4.5 %fusion.13 = bf16[1,768,4096]{2,1,0:T(8,128)(2,1)} fusion(bf16[96,768]{1,0:T(8,128)(2,1)S(1)} %copy-done.4, bf16[96,4096]{1,0:T(8,128)(2,1)S(1)} %reshape.73), kind=kOutput, calls=%fused_computation.16 | convolution fusion | flops 607125504 | bytes 7225344 | tf_op jit(solution)/shard_map/dot_general | solution.py:19
  177.5 19.4 %all-reduce.6.cloned.1.call-done = (bf16[8,4096]{1,0:T(8,128)(2,1)}, bf16[8,4096]{1,0:T(8,128)(2,1)}) async-done(((bf16[8,4096]{1,0:T(8,128)(2,1)}, bf16[8,4096]{1,0:T(8,128)(2,1)}), (bf16[8,4096]{1,0:T(8,128)(2,1)}, bf16[8,4096]{1,0:T(8,128)(2,1)})) %all-reduce.6.cloned.1.call-update) | async-done | bytes 131088
  196.8 1.5 constant_dynamic-slice_fusion
  (66 shorter events, 14.5 us)
Async XLA Ops:
  22.4 0.7 copy-start.10
  23.1 73.4 %copy-start.7 = (f32[8,96]{1,0:T(8,128)}, f32[8,96]{1,0:T(8,128)S(1)}, u32[]{:S(2)}) copy-start(f32[8,96]{1,0:T(8,128)S(1)} %get-tuple-element.6) | copy-start | bytes 9220
  55.1 10.8 %slice-start = ((s8[6291456]{0:T(1024)(128)(4,1)}), s8[4194304]{0:T(1024)(128)(4,1)S(1)}, s32[]{:S(2)}) async-start(s8[6291456]{0:T(1024)(128)(4,1)} %bitcast.64), calls=%async_computation.5 | async-start | bytes 8388608
  60.2 5.7 %slice-start.1 = ((s8[6291456]{0:T(1024)(128)(4,1)}), s8[2097152]{0:T(1024)(128)(4,1)S(1)}, s32[]{:S(2)}) async-start(s8[6291456]{0:T(1024)(128)(4,1)} %bitcast.64), calls=%async_computation.6 | async-start | bytes 4194304
  65.9 7.5 %copy-start.9 = (bf16[4,4096]{1,0:T(4,128)(2,1)S(1)}, bf16[4,4096]{1,0:T(4,128)(2,1)}, u32[]{:S(2)}) copy-start(bf16[4,4096]{1,0:T(4,128)(2,1)} %param.8) | copy-start | bytes 98308
  68.3 28.0 %all-to-all-start.1 = ((bf16[16,6,4096]{2,1,0:T(8,128)(2,1)}), bf16[16,6,4096]{2,1,0:T(8,128)(2,1)S(1)}, u32[]{:S(2)}, u32[]{:S(2)}) async-start(bf16[16,6,4096]{2,1,0:T(8,128)(2,1)} %reshape.74), calls=%async_computation.1 | async-start | bytes 2097152 | tf_op jit(solution)/shard_map/all_to_all | solution.py:133
  96.5 1.0 copy-start
  98.8 39.4 %slice-start.2 = ((s8[6291456]{0:T(1024)(128)(4,1)}), s8[2097152]{0:T(1024)(128)(4,1)S(1)}, s32[]{:S(2)}) async-start(s8[6291456]{0:T(1024)(128)(4,1)} %bitcast.66), calls=%async_computation.7 | async-start | bytes 4194304
  133.0 5.3 %slice-start.3 = ((s8[6291456]{0:T(1024)(128)(4,1)}), s8[4194304]{0:T(1024)(128)(4,1)S(1)}, s32[]{:S(2)}) async-start(s8[6291456]{0:T(1024)(128)(4,1)} %bitcast.66), calls=%async_computation.8 | async-start | bytes 8388608
  138.2 1.2 copy-start.5
  138.2 4.1 %copy-start.3 = (bf16[96,768]{1,0:T(8,128)(2,1)}, bf16[96,768]{1,0:T(8,128)(2,1)S(1)}, u32[]{:S(2)}) copy-start(bf16[96,768]{1,0:T(8,128)(2,1)S(1)} %get-tuple-element.13) | copy-start | bytes 442372
  138.2 2.3 %slice-start.4 = ((s8[6291456]{0:T(1024)(128)(4,1)}), s8[4194304]{0:T(1024)(128)(4,1)S(1)}, s32[]{:S(2)}) async-start(s8[6291456]{0:T(1024)(128)(4,1)} %bitcast.68), calls=%async_computation.9 | async-start | bytes 8388608
  138.3 2.9 %slice-start.5 = ((s8[6291456]{0:T(1024)(128)(4,1)}), s8[2097152]{0:T(1024)(128)(4,1)S(1)}, s32[]{:S(2)}) async-start(s8[6291456]{0:T(1024)(128)(4,1)} %bitcast.68), calls=%async_computation.10 | async-start | bytes 4194304
  141.2 17.9 %copy-start.1 = (bf16[96,4096]{1,0:T(8,128)(2,1)S(1)}, bf16[96,4096]{1,0:T(8,128)(2,1)}, u32[]{:S(2)}) copy-start(bf16[96,4096]{1,0:T(8,128)(2,1)} %copy-done) | copy-start | bytes 2359300
  141.2 19.7 %copy-start.2 = (bf16[96,4096]{1,0:T(8,128)(2,1)S(1)}, bf16[96,4096]{1,0:T(8,128)(2,1)}, u32[]{:S(2)}) copy-start(bf16[96,4096]{1,0:T(8,128)(2,1)} %reshape.78) | copy-start | bytes 2359300
  143.6 27.9 %all-to-all-start.3 = ((bf16[16,6,4096]{2,1,0:T(8,128)(2,1)}), bf16[16,6,4096]{2,1,0:T(8,128)(2,1)S(1)}, u32[]{:S(2)}, u32[]{:S(2)}) async-start(bf16[16,6,4096]{2,1,0:T(8,128)(2,1)} %reshape.79), calls=%async_computation.3 | async-start | bytes 2097152 | tf_op jit(solution)/shard_map/all_to_all | solution.py:140
  148.6 48.2 %all-reduce.6.cloned.1.call-start = ((), (), s32[]{:S(2)}) async-start(), calls=%async_computation.4 | async-start | bytes 262144
  157.8 7.6 %copy-start.6 = (bf16[96,768]{1,0:T(8,128)(2,1)S(1)}, bf16[96,768]{1,0:T(8,128)(2,1)}, u32[]{:S(2)}) copy-start(bf16[96,768]{1,0:T(8,128)(2,1)} %copy-done.5) | copy-start | bytes 442372
  165.4 6.4 %copy-start.8 = (f32[8,96]{1,0:T(8,128)S(1)}, f32[8,96]{1,0:T(8,128)}, u32[]{:S(2)}) copy-start(f32[8,96]{1,0:T(8,128)} %copy-done.7) | copy-start | bytes 9220
  165.4 7.5 %copy-start.4 = (bf16[96,768]{1,0:T(8,128)(2,1)S(1)}, bf16[96,768]{1,0:T(8,128)(2,1)}, u32[]{:S(2)}) copy-start(bf16[96,768]{1,0:T(8,128)(2,1)} %copy-done.3) | copy-start | bytes 442372
Sparse Core Ops, SparseCore 0:
  173.0 23.7 all-reduce.5
where the time goes:
time: 206 us; the launch traced here: 205 us
  blocking collectives  87.9 us (43%)
  waiting for transfers between devices  39.1 us (19%)
  matrix products  38.5 us (19%)
  between operations  14.9 us (7%)
  local copies, waits for them, and re-layouts  11.9 us (6%)
  starting transfers between devices  10 us (5%)
  other arithmetic  2.93 us (1%)
    all_to_all x1, blocking collectives, body(): lax.all_to_all(g_slots.reshape(experts, group_cap, feature_dim), 'expert'...  31.9 us
    all_to_all x1, blocking collectives, body(): lax.all_to_all(x_slots.reshape(experts, group_cap, feature_dim), 'expert'...  31.1 us
    unnamed x2, waiting for transfers between devices  19.4 us
    all_to_all x1, waiting for transfers between devices, body(): lax.all_to_all(out_part.reshape(experts, group_cap, feature_dim), 'expert...  18 us
    dot_general x3, matrix products, contract_last(): lax.dot_general(left, right, (((1,), (1,)), ((), ())), preferred_element_...  15.9 us
    dot_general x5, matrix products, contract_first(): lax.dot_general(left, right, (((0,), (0,)), ((), ())), preferred_element_...  15 us
    unnamed x1, blocking collectives  5.61 us
    all_gather x1, blocking collectives, body(): group_routes = lax.all_gather(routes, 'dp', axis=0, tiled=True)  5.43 us
  transfers between devices with their start and end apart: 3, of which 3 were waited for; matrix products, arithmetic and copies ran while one was open for 10% of the time, Pallas kernels for 0%

commit v1 on v0

v1 whole, which is shorter than its diff:
```python
import functools

import jax
import jax.numpy as jnp
from jax import lax
from jax.experimental import pallas as pl
from jax.experimental.pallas import tpu as pltpu
from jax.sharding import PartitionSpec as P

MESH = pl.DeviceIdType.MESH
LANES = 128
VMEM_BYTES = 56 * 1024 * 1024


def contract_last(left, right):
    return lax.dot_general(
        left, right, (((1,), (1,)), ((), ())), preferred_element_type=jnp.float32
    )


def contract_first(left, right):
    return lax.dot_general(
        left, right, (((0,), (0,)), ((), ())), preferred_element_type=jnp.float32
    )


class Place:
    def __init__(self, groups, hi):
        self.groups, self.hi = groups, hi
        self.d = lax.axis_index("dp")
        e = lax.axis_index("expert")
        self.z, self.u, self.v = e // 4, (e // 2) % 2, e % 2

    def at(self, d=None, z=None, u=None, v=None):
        d = self.d if d is None else d
        z = self.z if z is None else z
        u = self.u if u is None else u
        v = self.v if v is None else v
        return (d, (z * 2 + u) * 2 + v)

    def peers(self):
        found = [self.at(z=(self.z + k) % self.hi) for k in range(1, self.hi)]
        found += [self.at(d=(self.d + k) % self.groups) for k in range(1, self.groups)]
        return found + [self.at(u=1 - self.u), self.at(v=1 - self.v)]


def greet(place):
    barrier = pltpu.get_barrier_semaphore()
    peers = place.peers()
    for peer in peers:
        pl.semaphore_signal(barrier, inc=1, device_id=peer, device_id_type=MESH)
    pl.semaphore_wait(barrier, len(peers))


class Sender:
    def __init__(self, send, recv):
        self.send, self.recv, self.used = send, recv, 0

    def start(self, src, dst, peer):
        slot = self.used
        self.used += 1
        copy = pltpu.make_async_remote_copy(
            src_ref=src,
            dst_ref=dst,
            send_sem=self.send.at[slot],
            recv_sem=self.recv.at[slot],
            device_id=peer,
            device_id_type=MESH,
        )
        copy.start()
        return copy


def gather_kernel(groups, hi, x_ref, y_ref, m_ref, xo, yo, mo, send, recv, local):
    p = Place(groups, hi)
    d, z, u, v = p.d, p.z, p.u, p.v
    greet(p)
    sender = Sender(send, recv)
    trio = ((x_ref, xo), (m_ref, mo), (y_ref, yo))
    first = []
    for k in range(1, hi):
        for src, out in trio:
            first.append(sender.start(src, out.at[v, u, d, z], p.at(z=(z + k) % hi)))
    own = []
    for i, (src, out) in enumerate(trio):
        copy = pltpu.make_async_copy(src, out.at[v, u, d, z], local.at[i])
        copy.start()
        own.append(copy)
    for copy in own:
        copy.wait()
    for copy in first:
        copy.wait_recv()
    second, last = [], []
    for out in (xo, mo):
        block = out.at[v, u, d]
        for k in range(1, groups):
            second.append(sender.start(block, block, p.at(d=(d + k) % groups)))
    block = yo.at[v, u, d]
    second.append(sender.start(block, block, p.at(u=1 - u)))
    for _, out in trio:
        block = out.at[v, u, d]
        last.append(sender.start(block, block, p.at(v=1 - v)))
    for copy in second:
        copy.wait_recv()
    third = []
    for out in (xo, mo):
        block = out.at[v, u]
        third.append(sender.start(block, block, p.at(u=1 - u)))
    block = yo.at[v, :, d]
    for k in range(1, groups):
        third.append(sender.start(block, block, p.at(d=(d + k) % groups)))
    for out in (xo, mo):
        for k in range(1, groups):
            block = out.at[v, u, (d + k) % groups]
            last.append(sender.start(block, block, p.at(v=1 - v)))
    block = yo.at[v, 1 - u, d]
    last.append(sender.start(block, block, p.at(v=1 - v)))
    for copy in third:
        copy.wait_recv()
    for out in (xo, mo):
        block = out.at[v, 1 - u]
        last.append(sender.start(block, block, p.at(v=1 - v)))
    for k in range(1, groups):
        block = yo.at[v, :, (d + k) % groups]
        last.append(sender.start(block, block, p.at(v=1 - v)))
    for copy in last:
        copy.wait_recv()
    for copy in first + second + third + last:
        copy.wait_send()


def gather_all(groups, hi, x, y, m):
    shape = (2, 2, groups, hi)
    copies = 3 * (hi - 1) + 2 * (2 * (groups - 1)) + 2 * (groups - 1) + 3 * 4 + 8
    vmem = pl.BlockSpec(memory_space=pltpu.VMEM)
    return pl.pallas_call(
        functools.partial(gather_kernel, groups, hi),
        out_shape=[jax.ShapeDtypeStruct(shape + a.shape, a.dtype) for a in (x, y, m)],
        in_specs=[vmem] * 3,
        out_specs=[vmem] * 3,
        scratch_shapes=[
            pltpu.SemaphoreType.DMA((copies,)),
            pltpu.SemaphoreType.DMA((copies,)),
            pltpu.SemaphoreType.DMA((3,)),
        ],
        compiler_params=pltpu.CompilerParams(
            collective_id=0, has_side_effects=True, vmem_limit_bytes=VMEM_BYTES
        ),
        name="gather_all",
    )(x, y, m)


def add_into(dst, terms, lead):
    total = 1
    for n in lead:
        total *= n

    def step(i, carry):
        index, rest = [], i
        for n in reversed(lead):
            index.insert(0, rest % n)
            rest = rest // n
        acc = terms[0][tuple(index)].astype(jnp.float32)
        for term in terms[1:]:
            acc = acc + term[tuple(index)].astype(jnp.float32)
        dst[tuple(index)] = acc.astype(dst.dtype)
        return carry

    lax.fori_loop(0, total, step, 0)


def scatter_kernel(groups, hi, *refs):
    ins, outs = refs[0:3], refs[3:6]
    work = [refs[6 + 7 * i : 13 + 7 * i] for i in range(3)]
    send, recv = refs[27:29]
    p = Place(groups, hi)
    d, z, u, v = p.d, p.z, p.u, p.v
    greet(p)
    sender = Sender(send, recv)
    copies = []
    stage1 = []
    for part, (r1, *_) in zip(ins, work):
        stage1.append(sender.start(part.at[1 - v], r1, p.at(v=1 - v)))
    stage2 = []
    for i, (part, (r1, s1, r2, *_)) in enumerate(zip(ins, work)):
        stage1[i].wait_recv()
        add_into(s1, (part.at[v], r1), (2, groups, hi))
        if i == 1:
            stage2.append(
                [
                    sender.start(s1.at[:, (d + k) % groups], r2.at[k - 1], p.at(d=(d + k) % groups))
                    for k in range(1, groups)
                ]
            )
        else:
            stage2.append([sender.start(s1.at[1 - u], r2, p.at(u=1 - u))])
    stage3 = []
    for i, (r1, s1, r2, s2, r3, s3, r4) in enumerate(work):
        for copy in stage2[i]:
            copy.wait_recv()
        if i == 1:
            terms = [s1.at[:, d]] + [r2.at[k - 1] for k in range(1, groups)]
            add_into(s2, terms, (2, hi))
            stage3.append([sender.start(s2.at[1 - u], r3, p.at(u=1 - u))])
        else:
            add_into(s2, (s1.at[u], r2), (groups, hi))
            stage3.append(
                [
                    sender.start(s2.at[(d + k) % groups], r3.at[k - 1], p.at(d=(d + k) % groups))
                    for k in range(1, groups)
                ]
            )
    stage4 = []
    for i, (r1, s1, r2, s2, r3, s3, r4) in enumerate(work):
        for copy in stage3[i]:
            copy.wait_recv()
        if i == 1:
            add_into(s3, (s2.at[u], r3), (hi,))
        else:
            add_into(s3, [s2.at[d]] + [r3.at[k - 1] for k in range(1, groups)], (hi,))
        stage4.append(
            [
                sender.start(s3.at[(z + k) % hi], r4.at[k - 1], p.at(z=(z + k) % hi))
                for k in range(1, hi)
            ]
        )
    for i, (r1, s1, r2, s2, r3, s3, r4) in enumerate(work):
        for copy in stage4[i]:
            copy.wait_recv()
        acc = s3[z].astype(jnp.float32)
        for k in range(1, hi):
            acc = acc + r4[k - 1].astype(jnp.float32)
        outs[i][...] = acc.astype(outs[i].dtype)
    for copy in stage1 + sum(stage2 + stage3 + stage4, []):
        copy.wait_send()


def scatter_all(groups, hi, parts):
    scratch = []
    for i, part in enumerate(parts):
        tail = part.shape[4:]
        by_u = i != 1
        shapes = [
            (2, groups, hi),
            (2, groups, hi),
            (groups, hi) if by_u else (groups - 1, 2, hi),
            (groups, hi) if by_u else (2, hi),
            (groups - 1, hi) if by_u else (hi,),
            (hi,),
            (hi - 1,),
        ]
        scratch += [pltpu.VMEM(s + tail, part.dtype) for s in shapes]
    copies = 3 * (groups + 1 + hi)
    vmem = pl.BlockSpec(memory_space=pltpu.VMEM)
    return pl.pallas_call(
        functools.partial(scatter_kernel, groups, hi),
        out_shape=[jax.ShapeDtypeStruct(a.shape[4:], a.dtype) for a in parts],
        in_specs=[vmem] * 3,
        out_specs=[vmem] * 3,
        scratch_shapes=scratch
        + [pltpu.SemaphoreType.DMA((copies,)), pltpu.SemaphoreType.DMA((copies,))],
        compiler_params=pltpu.CompilerParams(
            collective_id=1, has_side_effects=True, vmem_limit_bytes=VMEM_BYTES
        ),
        name="scatter_all",
    )(*parts)


def body(tokens, grad_output, routes, gate_weights, gate_proj, up_proj, down_proj):
    experts = lax.axis_size("expert")
    groups = lax.axis_size("dp")
    hi = experts // 4
    token_count, feature_dim = tokens.shape
    me = lax.axis_index("expert")
    gate_local, up_local, down_local = gate_proj[0], up_proj[0], down_proj[0]
    lanes = jnp.arange(LANES, dtype=jnp.int32)
    chosen = routes[:, :, None] == lanes[None, None, :]
    dense = jnp.sum(jnp.where(chosen, gate_weights[:, :, None], 0.0), axis=1)
    x_all, dy_all, dense_all = gather_all(groups, hi, tokens, grad_output, dense)
    lead = x_all.shape[:5]
    x_rows = x_all.reshape(-1, feature_dim)
    dy_rows = dy_all.reshape(-1, feature_dim)
    mine = (lanes == me)[None, :]
    gate = jnp.sum(jnp.where(mine, dense_all.reshape(-1, LANES), 0.0), axis=1, keepdims=True)

    pre_gate = contract_last(x_rows, gate_local)
    pre_up = contract_last(x_rows, up_local)
    raw = contract_last(dy_rows, down_local)
    squash = jax.nn.sigmoid(pre_gate)
    active = pre_gate * squash
    slope = squash * (1.0 + pre_gate * (1.0 - squash))
    hidden = active * pre_up
    inner = jnp.sum(hidden * raw, axis=1, keepdims=True)
    hidden_g = (gate * hidden).astype(jnp.bfloat16)
    d_hidden = gate * raw
    d_upper = (d_hidden * active).astype(jnp.bfloat16)
    d_lower = (d_hidden * pre_up * slope).astype(jnp.bfloat16)
    out_part = jnp.dot(hidden_g, down_local, preferred_element_type=jnp.float32)
    back_part = jnp.dot(d_lower, gate_local, preferred_element_type=jnp.float32) + jnp.dot(
        d_upper, up_local, preferred_element_type=jnp.float32
    )
    inner_part = jnp.where(mine, inner, 0.0)
    layer_out, grad_tokens, inner_sum = scatter_all(
        groups,
        hi,
        (
            out_part.astype(jnp.bfloat16).reshape(lead + (feature_dim,)),
            back_part.astype(jnp.bfloat16).reshape(lead + (feature_dim,)),
            inner_part.reshape(lead + (LANES,)),
        ),
    )
    grad_gates = jnp.sum(jnp.where(chosen, inner_sum[:, None, :], 0.0), axis=2)
    return (
        layer_out,
        grad_tokens,
        grad_gates,
        contract_first(d_lower, x_rows).astype(jnp.bfloat16)[None],
        contract_first(d_upper, x_rows).astype(jnp.bfloat16)[None],
        contract_first(hidden_g, dy_rows).astype(jnp.bfloat16)[None],
    )


def solution(mesh):
    row = P(("dp", "expert"), None)
    weight = P("expert", "dp", None)
    return jax.shard_map(
        body,
        mesh=mesh,
        in_specs=(row,) * 4 + (weight,) * 3,
        out_specs=(row,) * 3 + (weight,) * 3,
        check_vma=False,
    )
```

time: 206 us -> 107 us (0.52)
  blocking collectives: 87.9 us -> 0 us
  Pallas kernels: 0 us -> 53.8 us
  waiting for transfers between devices: 39.1 us -> 0 us
  between operations: 14.9 us -> 0.76 us
  starting transfers between devices: 10 us -> 0 us
  local copies, waits for them, and re-layouts: 11.9 us -> 7.78 us
    all_to_all x2 -> x0, blocking collectives: 63 us -> none  [the longest x1 31.9 us: body(): lax.all_to_all(g_slots.reshape(experts, group_cap, feature_dim), 'expert'...]
    pallas_call x0 -> x2, Pallas kernels: none -> 53.8 us  [the longest x1 27 us: scatter_all(): pl.pallas_call(functools.partial(scatter_kernel, groups, hi), out_shape=[...]
    all_to_all x2 -> x0, waiting for transfers between devices: 19.7 us -> none  [the longest x1 18 us: body(): lax.all_to_all(out_part.reshape(experts, group_cap, feature_dim), 'expert...]
    unnamed x2 -> x0, waiting for transfers between devices: 19.4 us -> none
    all_gather x4 -> x0, blocking collectives: 19.3 us -> none  [the longest x1 5.43 us: body(): group_routes = lax.all_gather(routes, 'dp', axis=0, tiled=True)]
    all_to_all x2 -> x0, starting transfers between devices: 10 us -> none  [the longest x1 5 us: body(): lax.all_to_all(out_part.reshape(experts, group_cap, feature_dim), 'expert...]
    unnamed x1 -> x0, blocking collectives: 5.61 us -> none
    unnamed x38 -> x20, local copies, waits for them, and re-layouts: 4.7 us -> 1.33 us
  transfers between devices with their start and end apart: 3 -> 0, of which waited for: 3 -> 0; matrix products, arithmetic and copies ran while one was open for 10% -> 0% of each run, Pallas kernels for 0% -> 0%
where the time goes in v1:
time: 107 us
  Pallas kernels  53.8 us (50%)
  matrix products  40.2 us (38%)
  local copies, waits for them, and re-layouts  7.78 us (7%)
  other arithmetic  4.46 us (4%)
    pallas_call x1, Pallas kernels, scatter_all(): pl.pallas_call(functools.partial(scatter_kernel, groups, hi), out_shape=[...  27 us
    pallas_call x1, Pallas kernels, gather_all(): pl.pallas_call(functools.partial(gather_kernel, groups, hi), out_shape=[j...  26.8 us
    dot_general x3, matrix products, contract_first(): lax.dot_general(left, right, (((0,), (0,)), ((), ())), preferred_element_...  14.9 us
    dot_general x3, matrix products, contract_last(): lax.dot_general(left, right, (((1,), (1,)), ((), ())), preferred_element_...  14.6 us
    dot_general x1, matrix products, body(): out_part = jnp.dot(hidden_g, down_local, preferred_element_type=jnp.float32)  4.75 us
    dot_general x1, matrix products, body(): jnp.dot(d_upper, up_local, preferred_element_type=jnp.float32)  3.92 us
    reshape x1, local copies, waits for them, and re-layouts, body(): out_part.astype(jnp.bfloat16).reshape(lead + (feature_dim,))  2.39 us
    reshape x1, local copies, waits for them, and re-layouts, body(): back_part.astype(jnp.bfloat16).reshape(lead + (feature_dim,))  2.24 us

profile of v1, /device:TPU:0, one launch (start us, length us, event | category | flops | bytes accessed | tf_op | source)
XLA Modules:
  0.0 107.0 jit_solution(15926351332678138917)
XLA Ops:
  0.6 1.4 %select_reduce_fusion.2.m_ref = f32[4,128]{1,0:T(4,128)} fusion(f32[4,8]{1,0:T(4,128)} %param.10, s32[4,8]{1,0:T(4,128)} %param.9), kind=kLoop, calls=%fused_computation.30 | loop fusion | flops 11776 | bytes 2304 | tf_op jit(solution)/shard_map/reduce_sum | solution.py:278
  2.0 26.8 %gather_all.1 = (bf16[2,2,2,4,4,4096]{5,4,3,2,1,0:T(4,128)(2,1)}, bf16[2,2,2,4,4,4096]{5,4,3,2,1,0:T(4,128)(2,1)}, f32[2,2,2,4,4,128]{5,4,3,2,1,0:T(4,128)}) custom-call(bf16[4,4096]{1,0:T(4,128)(2,1)} %x_ref.1, bf16[4,4096]{1,0:T(4,128)(2,1)} %y_ref.1, f32[4,128]{1,0:T(4,128)} %select_reduce_fusion.2.m_ref), custom_call_target="tpu_custom_call" | custom-call | tf_op jit(solution)/shard_map/gather_all/pallas_call | solution.py:136
  28.8 1.0 select_reduce_fusion
  29.7 0.1 mul.40
  29.9 1.3 %reshape.52 = bf16[128,4096]{1,0:T(8,128)(2,1)S(1)} reshape(bf16[2,2,2,4,4,4096]{5,4,3,2,1,0:T(4,128)(2,1)} %get-tuple-element.13) | data formatting | bytes 2097152 | tf_op jit(solution)/shard_map/reshape | solution.py:281
  31.2 5.9 %fusion.6 = f32[128,768]{1,0:T(8,128)} fusion(bf16[128,4096]{1,0:T(8,128)(2,1)S(1)} %reshape.52, bf16[1,768,4096]{2,1,0:T(8,128)(2,1)} %param.12), kind=kOutput, calls=%fused_computation.9 | convolution fusion | flops 805306368 | bytes 7733248 | tf_op jit(solution)/shard_map/dot_general | solution.py:16
  37.1 3.0 %fusion.10 = f32[128,768]{1,0:T(8,128)} fusion(bf16[128,4096]{1,0:T(8,128)(2,1)S(1)} %reshape.52, bf16[1,768,4096]{2,1,0:T(8,128)(2,1)S(1)} %copy-done), kind=kOutput, calls=%fused_computation.13 | convolution fusion | flops 805306368 | bytes 7733248 | tf_op jit(solution)/shard_map/dot_general | solution.py:16
  40.2 0.3 reshape.54
  40.4 5.6 %multiply_reduce_fusion = (f32[128]{0:T(128)S(1)}, bf16[128,768]{1,0:T(8,128)(2,1)S(1)}, bf16[128,768]{1,0:T(8,128)(2,1)S(1)}, bf16[128,768]{1,0:T(8,128)(2,1)S(1)}) fusion(f32[128,768]{1,0:T(8,128)} %fusion.6, f32[128,768]{1,0:T(8,128)} %fusion.10, f32[128]{0:T(128)S(1)} %mul.40, bf16[128,4096]{1,0:T(8,128)(2,1)S(1)} %reshape.54, ...), kind=kOutput, calls=%fused_computation.21 | convolution fusion | flops 807174016 | bytes 8717312 | tf_op jit(solution)/shard_map/dot_general | solution.py:16
  46.1 0.1 broadcast_in_dim.72
  46.2 0.7 broadcast_select_fusion.refs_2_
  46.9 4.7 %fusion.21 = bf16[128,4096]{1,0:T(8,128)(2,1)} fusion(bf16[128,768]{1,0:T(8,128)(2,1)S(1)} %get-tuple-element.20, bf16[1,768,4096]{2,1,0:T(8,128)(2,1)} %param.13), kind=kOutput, calls=%fused_computation.20 | convolution fusion | flops 805830656 | bytes 7536640 | tf_op jit(solution)/shard_map/dot_general | solution.py:298
  51.7 2.4 %reshape.53.refs_0_ = bf16[2,2,2,4,4,4096]{5,4,3,2,1,0:T(4,128)(2,1)} reshape(bf16[128,4096]{1,0:T(8,128)(2,1)} %fusion.21) | data formatting | bytes 2097152 | tf_op jit(solution)/shard_map/reshape | solution.py:307
  54.1 3.9 %fusion.4 = f32[128,4096]{1,0:T(8,128)S(1)} fusion(bf16[128,768]{1,0:T(8,128)(2,1)S(1)} %get-tuple-element.21, bf16[1,768,4096]{2,1,0:T(8,128)(2,1)} %param.12), kind=kOutput, calls=%fused_computation.7 | convolution fusion | flops 805306368 | bytes 8585216 | tf_op jit(solution)/shard_map/dot_general | solution.py:299
  58.0 0.1 slice-done.1
  58.1 2.1 %fusion.18 = bf16[128,4096]{1,0:T(8,128)(2,1)} fusion(f32[128,4096]{1,0:T(8,128)S(1)} %fusion.4, bf16[128,768]{1,0:T(8,128)(2,1)S(1)} %get-tuple-element.19, bf16[1,768,4096]{2,1,0:T(8,128)(2,1)S(1)} %bitcast.42), kind=kOutput, calls=%fused_computation.19 | convolution fusion | flops 806354944 | bytes 9633792 | tf_op jit(solution)/shard_map/dot_general | solution.py:299
  60.1 2.2 %reshape.55.refs_1_ = bf16[2,2,2,4,4,4096]{5,4,3,2,1,0:T(4,128)(2,1)} reshape(bf16[128,4096]{1,0:T(8,128)(2,1)} %fusion.18) | data formatting | bytes 2097152 | tf_op jit(solution)/shard_map/reshape | solution.py:308
  62.4 27.0 %scatter_all.1 = (bf16[4,4096]{1,0:T(4,128)(2,1)}, bf16[4,4096]{1,0:T(4,128)(2,1)}, f32[4,128]{1,0:T(4,128)}) custom-call(bf16[2,2,2,4,4,4096]{5,4,3,2,1,0:T(4,128)(2,1)} %reshape.53.refs_0_, bf16[2,2,2,4,4,4096]{5,4,3,2,1,0:T(4,128)(2,1)} %reshape.55.refs_1_, f32[2,2,2,4,4,128]{5,4,3,2,1,0:T(4,128)} %broadcast_select_fusion.refs_2_), custom_call_target="tpu_custom_call" | custom-call | tf_op jit(solution)/shard_map/scatter_all/pallas_call | solution.py:255
  89.4 1.4 %select_reduce_fusion.1 = f32[4,8]{1,0:T(4,128)} fusion(f32[4,128]{1,0:T(4,128)} %get-tuple-element.17, s32[4,8]{1,0:T(4,128)S(1)} %copy-done.6), kind=kLoop, calls=%fused_computation.29 | loop fusion | flops 12256 | bytes 2304 | tf_op jit(solution)/shard_map/reduce_sum | solution.py:312
  90.9 5.9 %fusion.14 = bf16[1,768,4096]{2,1,0:T(8,128)(2,1)} fusion(bf16[128,768]{1,0:T(8,128)(2,1)} %copy-done.2, bf16[128,4096]{1,0:T(8,128)(2,1)} %copy-done.1), kind=kOutput, calls=%fused_computation.17 | convolution fusion | flops 808452096 | bytes 7536640 | tf_op jit(solution)/shard_map/dot_general | solution.py:22
  96.7 4.5 %fusion.12 = bf16[1,768,4096]{2,1,0:T(8,128)(2,1)} fusion(bf16[128,768]{1,0:T(8,128)(2,1)S(1)} %get-tuple-element.19, bf16[128,4096]{1,0:T(8,128)(2,1)S(1)} %reshape.52), kind=kOutput, calls=%fused_computation.15 | convolution fusion | flops 808452096 | bytes 7536640 | tf_op jit(solution)/shard_map/dot_general | solution.py:22
  101.2 4.5 %fusion.13 = bf16[1,768,4096]{2,1,0:T(8,128)(2,1)} fusion(bf16[128,768]{1,0:T(8,128)(2,1)S(1)} %get-tuple-element.21, bf16[128,4096]{1,0:T(8,128)(2,1)S(1)} %reshape.52), kind=kOutput, calls=%fused_computation.16 | convolution fusion | flops 808452096 | bytes 7536640 | tf_op jit(solution)/shard_map/dot_general | solution.py:22
  105.8 0.6 copy.15
  106.4 0.6 copy.16
  (19 shorter events, 0.0 us)
Async XLA Ops:
  31.2 5.9 %copy-start = (bf16[1,768,4096]{2,1,0:T(8,128)(2,1)S(1)}, bf16[1,768,4096]{2,1,0:T(8,128)(2,1)}, u32[]{:S(2)}) copy-start(bf16[1,768,4096]{2,1,0:T(8,128)(2,1)} %param.11) | copy-start | bytes 18874372
  31.2 8.9 %copy-start.3 = (bf16[2,2,2,4,4,4096]{5,4,3,2,1,0:T(4,128)(2,1)S(1)}, bf16[2,2,2,4,4,4096]{5,4,3,2,1,0:T(4,128)(2,1)}, u32[]{:S(2)}) copy-start(bf16[2,2,2,4,4,4096]{5,4,3,2,1,0:T(4,128)(2,1)} %get-tuple-element.14) | copy-start | bytes 3145732
  40.4 6.5 %copy-start.1 = (bf16[128,4096]{1,0:T(8,128)(2,1)}, bf16[128,4096]{1,0:T(8,128)(2,1)S(1)}, u32[]{:S(2)}) copy-start(bf16[128,4096]{1,0:T(8,128)(2,1)S(1)} %reshape.54) | copy-start | bytes 3145732
  46.1 0.9 copy-start.2
  51.7 6.3 %slice-start = ((s8[6291456]{0:T(1024)(128)(4,1)}), s8[2097152]{0:T(1024)(128)(4,1)S(1)}, s32[]{:S(2)}) async-start(s8[6291456]{0:T(1024)(128)(4,1)} %bitcast.41), calls=%async_computation | async-start | bytes 4194304
  54.1 4.0 %slice-start.1 = ((s8[6291456]{0:T(1024)(128)(4,1)}), s8[4194304]{0:T(1024)(128)(4,1)S(1)}, s32[]{:S(2)}) async-start(s8[6291456]{0:T(1024)(128)(4,1)} %bitcast.41), calls=%async_computation.1 | async-start | bytes 8388608
  58.1 31.4 %copy-start.6 = (s32[4,8]{1,0:T(4,128)S(1)}, s32[4,8]{1,0:T(4,128)}, u32[]{:S(2)}) copy-start(s32[4,8]{1,0:T(4,128)} %param.9) | copy-start | bytes 388
  96.7 9.1 %copy-start.5 = (bf16[4,4096]{1,0:T(4,128)(2,1)S(1)}, bf16[4,4096]{1,0:T(4,128)(2,1)}, u32[]{:S(2)}) copy-start(bf16[4,4096]{1,0:T(4,128)(2,1)} %get-tuple-element.28) | copy-start | bytes 98308
  96.7 9.7 %copy-start.4 = (bf16[4,4096]{1,0:T(4,128)(2,1)S(1)}, bf16[4,4096]{1,0:T(4,128)(2,1)}, u32[]{:S(2)}) copy-start(bf16[4,4096]{1,0:T(4,128)(2,1)} %get-tuple-element.29) | copy-start | bytes 98308

commit v2 on v1

v2 whole, which is shorter than its diff:
```python
import functools

import jax
import jax.numpy as jnp
from jax import lax
from jax.experimental import pallas as pl
from jax.experimental.pallas import tpu as pltpu
from jax.sharding import PartitionSpec as P

MESH = pl.DeviceIdType.MESH
LANES = 128
UNIT = 8
CHUNKS = 4
VMEM_BYTES = 62 * 1024 * 1024


class Place:
    def __init__(self, groups, hi):
        self.groups, self.hi = groups, hi
        self.d = lax.axis_index("dp")
        e = lax.axis_index("expert")
        self.z, self.u, self.v = e // 4, (e // 2) % 2, e % 2

    def at(self, d=None, z=None, u=None, v=None):
        d = self.d if d is None else d
        z = self.z if z is None else z
        u = self.u if u is None else u
        v = self.v if v is None else v
        return (d, (z * 2 + u) * 2 + v)

    def peers(self):
        found = [self.at(z=(self.z + k) % self.hi) for k in range(1, self.hi)]
        found += [self.at(d=(self.d + k) % self.groups) for k in range(1, self.groups)]
        return found + [self.at(u=1 - self.u), self.at(v=1 - self.v)]


def greet(place):
    barrier = pltpu.get_barrier_semaphore()
    peers = place.peers()
    for peer in peers:
        pl.semaphore_signal(barrier, inc=1, device_id=peer, device_id_type=MESH)
    pl.semaphore_wait(barrier, len(peers))


class Sender:
    def __init__(self, send, recv):
        self.send, self.recv, self.used = send, recv, 0

    def start(self, src, dst, peer):
        slot = self.used
        self.used += 1
        copy = pltpu.make_async_remote_copy(
            src_ref=src,
            dst_ref=dst,
            send_sem=self.send.at[slot],
            recv_sem=self.recv.at[slot],
            device_id=peer,
            device_id_type=MESH,
        )
        copy.start()
        return copy


def wait_all(copies):
    for copy in copies:
        copy.wait_recv()


def gather(p, sender, sources):
    groups, hi = p.groups, p.hi
    d, z, u, v = p.d, p.z, p.u, p.v
    every = []

    def send(src, dst, peer):
        copy = sender.start(src, dst, peer)
        every.append(copy)
        return copy

    first = []
    for src, out, cols, _ in sources:
        first.append(
            [
                send(src.at[:, cols], out.at[v, u, d, z, :, cols], p.at(z=(z + k) % hi))
                for k in range(1, hi)
            ]
        )
    yield None
    second, third, last = [], [], []
    for i, (_, out, cols, u_first) in enumerate(sources):
        wait_all(first[i])
        block = out.at[v, u, d, :, :, cols]
        if u_first:
            second.append([send(block, block, p.at(u=1 - u))])
        else:
            second.append([send(block, block, p.at(d=(d + k) % groups)) for k in range(1, groups)])
        last.append(send(block, block, p.at(v=1 - v)))
    for i, (_, out, cols, u_first) in enumerate(sources):
        wait_all(second[i])
        if u_first:
            block = out.at[v, :, d, :, :, cols]
            third.append([send(block, block, p.at(d=(d + k) % groups)) for k in range(1, groups)])
            block = out.at[v, 1 - u, d, :, :, cols]
            last.append(send(block, block, p.at(v=1 - v)))
        else:
            block = out.at[v, u, :, :, :, cols]
            third.append([send(block, block, p.at(u=1 - u))])
            for k in range(1, groups):
                block = out.at[v, u, (d + k) % groups, :, :, cols]
                last.append(send(block, block, p.at(v=1 - v)))
    for i, (_, out, cols, u_first) in enumerate(sources):
        wait_all(third[i])
        if u_first:
            for k in range(1, groups):
                block = out.at[v, :, (d + k) % groups, :, :, cols]
                last.append(send(block, block, p.at(v=1 - v)))
        else:
            block = out.at[v, 1 - u, :, :, :, cols]
            last.append(send(block, block, p.at(v=1 - v)))
    wait_all(last)
    for copy in every:
        copy.wait_send()
    yield None


def add_to(dst, terms, lead):
    total = 1
    for n in lead:
        total *= n

    def step(i, carry):
        index, rest = [], i
        for n in reversed(lead):
            index.insert(0, rest % n)
            rest = rest // n
        at = tuple(index) + (slice(None), slice(None))
        acc = dst[at].astype(jnp.float32)
        for term in terms:
            acc = acc + term[at].astype(jnp.float32)
        dst[at] = acc.astype(dst.dtype)
        return carry

    lax.fori_loop(0, total, step, 0)


def scatter_steps(p, sender, every, buf, landing, out, cols, u_first):
    groups, hi = p.groups, p.hi
    d, z, u, v = p.d, p.z, p.u, p.v
    r1, ru, rd, r4 = landing

    def send(src, dst, peer):
        copy = sender.start(src, dst, peer)
        every.append(copy)
        return copy

    going = [send(buf.at[1 - v, :, :, :, :, cols], r1, p.at(v=1 - v))]
    yield None
    wait_all(going)
    mine = buf.at[v, :, :, :, :, cols]
    add_to(mine, [r1], (2, groups, hi))
    if u_first:
        going = [
            send(buf.at[v, 1 - u, :, :, :, cols], ru, p.at(u=1 - u))
        ]
    else:
        going = [
            send(
                buf.at[v, :, (d + k) % groups, :, :, cols],
                rd.at[k - 1],
                p.at(d=(d + k) % groups),
            )
            for k in range(1, groups)
        ]
    yield None
    wait_all(going)
    if u_first:
        add_to(buf.at[v, u, :, :, :, cols], [ru], (groups, hi))
        going = [
            send(
                buf.at[v, u, (d + k) % groups, :, :, cols],
                rd.at[k - 1, 0],
                p.at(d=(d + k) % groups),
            )
            for k in range(1, groups)
        ]
    else:
        terms = [rd.at[k - 1] for k in range(1, groups)]
        add_to(buf.at[v, :, d, :, :, cols], terms, (2, hi))
        going = [send(buf.at[v, 1 - u, d, :, :, cols], ru.at[0], p.at(u=1 - u))]
    yield None
    wait_all(going)
    if u_first:
        terms = [rd.at[k - 1, 0] for k in range(1, groups)]
    else:
        terms = [ru.at[0]]
    add_to(buf.at[v, u, d, :, :, cols], terms, (hi,))
    going = [
        send(buf.at[v, u, d, (z + k) % hi, :, cols], r4.at[k - 1], p.at(z=(z + k) % hi))
        for k in range(1, hi)
    ]
    yield None
    wait_all(going)
    acc = buf[v, u, d, z, :, cols].astype(jnp.float32)
    for k in range(1, hi):
        acc = acc + r4[k - 1].astype(jnp.float32)
    out[:, cols] = acc.astype(out.dtype)
    yield None


def dot(left, right, dims):
    return lax.dot_general(left, right, (dims, ((), ())), preferred_element_type=jnp.float32)


def layer_kernel(groups, hi, *refs):
    x_ref, m_ref, gate_hbm, up_hbm, down_hbm = refs[0:5]
    out_ref, inner_ref, z_ref, low_ref, upper_ref, hid_ref = refs[5:11]
    gate_w, up_w, down_w, buf, mbuf, inner_s = refs[11:17]
    landing = [refs[17 + 4 * c : 21 + 4 * c] for c in range(CHUNKS + 1)]
    send_sem, recv_sem, local = refs[21 + 4 * CHUNKS :]
    p = Place(groups, hi)
    d, z, u, v = p.d, p.z, p.u, p.v
    width = x_ref.shape[1]
    hidden_dim = gate_w.shape[0]
    rows = z_ref.shape[0]
    loads = []
    for i, (src, dst) in enumerate(((gate_hbm, gate_w), (up_hbm, up_w), (down_hbm, down_w))):
        copy = pltpu.make_async_copy(src, dst, local.at[i])
        copy.start()
        loads.append(copy)
    own = []
    for i, (src, dst) in enumerate(((x_ref, buf), (m_ref, mbuf))):
        copy = pltpu.make_async_copy(src, dst.at[v, u, d, z], local.at[3 + i])
        copy.start()
        own.append(copy)
    greet(p)
    sender = Sender(send_sem, recv_sem)
    span = width // CHUNKS
    cuts = [(slice(c * span, (c + 1) * span), c % 2 == 1) for c in range(CHUNKS)]
    sources = [(x_ref, buf, cols, order) for cols, order in cuts]
    sources.append((m_ref, mbuf, slice(0, LANES), False))
    moves = gather(p, sender, sources)
    next(moves)
    for copy in own:
        copy.wait()
    next(moves)

    def place_of(shard):
        rest = shard // hi
        return (rest // (2 * groups), (rest // groups) % 2, rest % groups, shard % hi)

    def pack(i, carry):
        both = [buf[place_of(2 * i + j)].astype(jnp.float32) for j in range(2)]
        at = pl.ds(pl.multiple_of(i * 2 * UNIT, 2 * UNIT), 2 * UNIT)
        z_ref[at, :] = jnp.concatenate(both, axis=0).astype(jnp.bfloat16)
        return carry

    lax.fori_loop(0, rows // (2 * UNIT), pack, 0)
    for copy in loads:
        copy.wait()

    me = lax.axis_index("expert")
    block = min(rows, 256)
    units = block // UNIT
    tile = 256 if hidden_dim % 256 == 0 else hidden_dim
    lane = lax.broadcasted_iota(jnp.int32, (1, LANES), 1)

    def forward(i, carry):
        at = pl.ds(pl.multiple_of(i * block, block), block)
        planes = [mbuf[place_of(i * units + j)] for j in range(units)]
        dense = jnp.concatenate(planes, axis=0)
        gate = jnp.sum(jnp.where(lane == me, dense, 0.0), axis=1, keepdims=True)
        inner_s[...] = jnp.zeros_like(inner_s)

        def hidden_tile(f, c):
            if tile == hidden_dim:
                fs = slice(0, hidden_dim)
            else:
                fs = pl.ds(pl.multiple_of(f * tile, tile), tile)
            pre_gate = dot(z_ref[at, :], gate_w[fs, :], ((1,), (1,)))
            pre_up = dot(z_ref[at, :], up_w[fs, :], ((1,), (1,)))
            raw = dot(z_ref[at, :], down_w[fs, :], ((1,), (1,)))
            raw = pltpu.roll(raw, block - UNIT // 2, 0)
            squash = 1.0 / (1.0 + jnp.exp(-pre_gate))
            active = pre_gate * squash
            slope = squash * (1.0 + pre_gate * (1.0 - squash))
            hidden = active * pre_up
            inner_s[:, 0:1] += jnp.sum(hidden * raw, axis=1, keepdims=True)
            hidden = gate * hidden
            d_hidden = gate * raw
            d_upper = d_hidden * active
            d_lower = d_hidden * pre_up * slope
            half = UNIT // 2
            hid_ref[at, fs] = hidden.astype(jnp.bfloat16)
            low_ref[at, fs] = pltpu.roll(d_lower, half, 0).astype(jnp.bfloat16)
            upper_ref[at, fs] = pltpu.roll(d_upper, half, 0).astype(jnp.bfloat16)
            return c

        lax.fori_loop(0, hidden_dim // tile, hidden_tile, 0)
        part = jnp.where(lane == me, inner_s[:, 0:1], 0.0)
        for j in range(units):
            mbuf[place_of(i * units + j)] = part[j * UNIT : (j + 1) * UNIT]
        return carry

    lax.fori_loop(0, rows // block, forward, 0)

    every = []
    lines = [
        scatter_steps(p, sender, every, mbuf, landing[CHUNKS], inner_ref, slice(0, LANES), True)
    ]
    step = 256

    def backward(base):
        def one(n, carry):
            i, n = n // (span // step), n % (span // step)
            at = pl.ds(pl.multiple_of(i * block, block), block)
            cs = pl.ds(pl.multiple_of(base + n * step, step), step)
            acc = dot(hid_ref[at, :], down_w[:, cs], ((1,), (0,)))
            acc = acc + dot(low_ref[at, :], gate_w[:, cs], ((1,), (0,)))
            acc = acc + dot(upper_ref[at, :], up_w[:, cs], ((1,), (0,)))
            for j in range(units):
                a, b, c, e = place_of(i * units + j)
                buf[a, b, c, e, :, cs] = acc[j * UNIT : (j + 1) * UNIT].astype(jnp.bfloat16)
            return carry

        lax.fori_loop(0, (rows // block) * (span // step), one, 0)

    next(lines[0])
    for t in range(CHUNKS + 4):
        if t < CHUNKS:
            cols, order = cuts[t]
            backward(t * span)
            fresh = scatter_steps(p, sender, every, buf, landing[t], out_ref, cols, order)
            lines.append(fresh)
            next(fresh)
        for line in lines[: t + 1]:
            next(line, None)
    for copy in every:
        copy.wait_send()


def layer(groups, hi, x, m, gate_local, up_local, down_local):
    lead = (2, 2, groups, hi)
    rows = 4 * groups * hi * UNIT
    hidden_dim, width = gate_local.shape
    half = jax.ShapeDtypeStruct((rows, hidden_dim), jnp.bfloat16)

    def landing(cols, dtype, u_first):
        return [
            pltpu.VMEM((2, groups, hi, UNIT, cols), dtype),
            pltpu.VMEM((groups if u_first else 1, hi, UNIT, cols), dtype),
            pltpu.VMEM((groups - 1, 1 if u_first else 2, hi, UNIT, cols), dtype),
            pltpu.VMEM((hi - 1, UNIT, cols), dtype),
        ]

    moved = CHUNKS + 1
    copies = moved * 2 * (hi - 1 + groups - 1 + 1 + 2 * groups + 4)
    vmem = pl.BlockSpec(memory_space=pltpu.VMEM)
    weight = pltpu.VMEM((hidden_dim, width), jnp.bfloat16)
    return pl.pallas_call(
        functools.partial(layer_kernel, groups, hi),
        out_shape=[
            jax.ShapeDtypeStruct((UNIT, width), jnp.bfloat16),
            jax.ShapeDtypeStruct((UNIT, LANES), jnp.float32),
            jax.ShapeDtypeStruct((rows, width), jnp.bfloat16),
            half,
            half,
            half,
        ],
        in_specs=[vmem] * 2 + [pl.BlockSpec(memory_space=pl.ANY)] * 3,
        out_specs=[vmem] * 6,
        scratch_shapes=[weight] * 3
        + [
            pltpu.VMEM(lead + (UNIT, width), jnp.bfloat16),
            pltpu.VMEM(lead + (UNIT, LANES), jnp.float32),
        ]
        + [pltpu.VMEM((min(rows, 256), LANES), jnp.float32)]
        + sum([landing(width // CHUNKS, jnp.bfloat16, c % 2 == 1) for c in range(CHUNKS)], [])
        + landing(LANES, jnp.float32, True)
        + [
            pltpu.SemaphoreType.DMA((copies,)),
            pltpu.SemaphoreType.DMA((copies,)),
            pltpu.SemaphoreType.DMA((5,)),
        ],
        compiler_params=pltpu.CompilerParams(
            collective_id=0, has_side_effects=True, vmem_limit_bytes=VMEM_BYTES
        ),
        name="layer",
    )(x, m, gate_local, up_local, down_local)


def grad_kernel(z_ref, low_ref, upper_ref, hid_ref, gate_out, up_out, down_out, turned):
    @pl.when(pl.program_id(0) == 0)
    def _():
        rows, half = low_ref.shape[0], UNIT // 2
        shifts = (rows - half, rows - half, half)
        for i, ref in enumerate((low_ref, upper_ref, hid_ref)):
            moved = pltpu.roll(ref[...].astype(jnp.float32), shifts[i], 0)
            turned[i] = moved.astype(jnp.bfloat16).T

    for i, out in enumerate((gate_out, up_out, down_out)):
        out[0] = dot(turned[i], z_ref[...], ((1,), (0,))).astype(jnp.bfloat16)


def weight_grads(z_rows, low, upper, hid):
    rows, width = z_rows.shape
    hidden_dim = low.shape[1]
    tile = 512
    whole = pl.BlockSpec((rows, hidden_dim), lambda n: (0, 0))
    out = pl.BlockSpec((1, hidden_dim, tile), lambda n: (0, 0, n))
    return pl.pallas_call(
        grad_kernel,
        grid=(width // tile,),
        out_shape=[jax.ShapeDtypeStruct((1, hidden_dim, width), jnp.bfloat16)] * 3,
        in_specs=[pl.BlockSpec((rows, tile), lambda n: (0, n)), whole, whole, whole],
        out_specs=[out] * 3,
        scratch_shapes=[pltpu.VMEM((3, hidden_dim, rows), jnp.bfloat16)],
        compiler_params=pltpu.CompilerParams(vmem_limit_bytes=VMEM_BYTES // 2),
        name="weight_grads",
    )(z_rows, low, upper, hid)


def body(tokens, grad_output, routes, gate_weights, gate_proj, up_proj, down_proj):
    experts = lax.axis_size("expert")
    groups = lax.axis_size("dp")
    hi = experts // 4
    token_count = tokens.shape[0]
    lanes = jnp.arange(LANES, dtype=jnp.int32)
    chosen = routes[:, :, None] == lanes[None, None, :]
    dense = jnp.sum(jnp.where(chosen, gate_weights[:, :, None], 0.0), axis=1)
    both = jnp.concatenate([tokens, grad_output], axis=0)
    dense = jnp.concatenate([dense, jnp.zeros_like(dense)], axis=0)
    sums, inner, z_rows, low, upper, hid = layer(
        groups, hi, both, dense, gate_proj[0], up_proj[0], down_proj[0]
    )
    grads = weight_grads(z_rows, low, upper, hid)
    inner = inner[:token_count]
    grad_gates = jnp.sum(jnp.where(chosen, inner[:, None, :], 0.0), axis=2)
    return (sums[:token_count], sums[token_count:], grad_gates, *grads)


def solution(mesh):
    row = P(("dp", "expert"), None)
    weight = P("expert", "dp", None)
    return jax.shard_map(
        body,
        mesh=mesh,
        in_specs=(row,) * 4 + (weight,) * 3,
        out_specs=(row,) * 3 + (weight,) * 3,
        check_vma=False,
    )
```

time: 107 us -> 91.3 us (0.85)
  matrix products: 40.2 us -> 0 us
  Pallas kernels: 53.8 us -> 79.8 us
  other arithmetic: 4.46 us -> 2.96 us
    dot_general x9 -> x0, matrix products: 40.2 us -> none  [the longest x3 14.9 us: contract_first(): lax.dot_general(left, right, (((0,), (0,)), ((), ())), preferred_element_...]
    pallas_call x2, Pallas kernels: 53.8 us -> 79.8 us  [the longest x1 71.6 us: layer(): pl.pallas_call(functools.partial(layer_kernel, groups, hi), out_shape=[ja...]
    reshape x4 -> x0, local copies, waits for them, and re-layouts: 6.23 us -> none  [the longest x1 2.39 us: body(): out_part.astype(jnp.bfloat16).reshape(lead + (feature_dim,))]
    unnamed x20 -> x10, local copies, waits for them, and re-layouts: 1.33 us -> 4.58 us
    slice x0 -> x2, local copies, waits for them, and re-layouts: none -> 2.25 us  [the longest x1 1.57 us: body(): return (sums[:token_count], sums[token_count:], grad_gates, *grads)]
    reduce_sum x2 -> x1, other arithmetic: 2.36 us -> 0.73 us  [body(): grad_gates = jnp.sum(jnp.where(chosen, inner[:, None, :], 0.0), axis=2)]
    concatenate x0 -> x1, other arithmetic: none -> 1.44 us  [body(): both = jnp.concatenate([tokens, grad_output], axis=0)]
where the time goes in v2:
time: 91.3 us; the launch traced here: 90.8 us
  Pallas kernels  79.8 us (87%)
  local copies, waits for them, and re-layouts  7.43 us (8%)
  other arithmetic  2.96 us (3%)
    pallas_call x1, Pallas kernels, layer(): pl.pallas_call(functools.partial(layer_kernel, groups, hi), out_shape=[ja...  71.6 us
    pallas_call x1, Pallas kernels, weight_grads(): pl.pallas_call(grad_kernel, grid=(width // tile,), out_shape=[jax.ShapeDt...  8.22 us
    unnamed x10, local copies, waits for them, and re-layouts  4.58 us

profile of v2, /device:TPU:0, one launch (start us, length us, event | category | flops | bytes accessed | tf_op | source)
XLA Modules:
  0.0 90.8 jit_solution(16229299236899430951)
XLA Ops:
  0.6 0.8 select_reduce_fusion.1
  1.4 0.6 concatenate.7.refs_1_
  2.0 1.4 %pad_maximum_fusion.refs_0_ = bf16[8,4096]{1,0:T(8,128)(2,1)} fusion(bf16[4,4096]{1,0:T(4,128)(2,1)} %param.8, bf16[4,4096]{1,0:T(4,128)(2,1)} %param.7), kind=kLoop, calls=%fused_computation | loop fusion | flops 131072 | bytes 131072 | tf_op jit(solution)/shard_map/concatenate | solution.py:429
  3.5 0.0 copy-start.4
  3.5 71.6 %layer.1 = (bf16[8,4096]{1,0:T(8,128)(2,1)}, f32[8,128]{1,0:T(8,128)}, bf16[256,4096]{1,0:T(8,128)(2,1)}, bf16[256,768]{1,0:T(8,128)(2,1)}, bf16[256,768]{1,0:T(8,128)(2,1)}, /*index=5*/bf16[256,768]{1,0:T(8,128)(2,1)}) custom-call(bf16[8,4096]{1,0:T(8,128)(2,1)} %pad_maximum_fusion.refs_0_, f32[8,128]{1,0:T(8,128)} %concatenate.7.refs_1_, ...), custom_call_target="tpu_custom_call" | custom-call | tf_op jit(solution)/shard_map/layer/pallas_call | solution.py:358
  75.0 1.6 %fusion = (bf16[4,4096]{1,0:T(4,128)(2,1)}, bf16[4,4096]{1,0:T(4,128)(2,1)}) fusion(bf16[8,4096]{1,0:T(8,128)(2,1)} %get-tuple-element.15), kind=kLoop, calls=%fused_computation.4 | loop fusion | bytes 131072 | tf_op jit(solution)/shard_map/slice | solution.py:437
  76.6 0.7 slice.11
  77.3 0.0 copy-done.4
  77.3 0.7 select_reduce_fusion
  78.0 0.0 copy-start
  78.0 1.6 %copy-done = bf16[256,4096]{1,0:T(8,128)(2,1)S(1)} copy-done((bf16[256,4096]{1,0:T(8,128)(2,1)S(1)}, bf16[256,4096]{1,0:T(8,128)(2,1)}, u32[]{:S(2)}) %copy-start) | copy-done | bytes 2097176
  79.6 0.0 copy-start.1
  79.6 1.0 %copy-done.1 = bf16[256,768]{1,0:T(8,128)(2,1)S(1)} copy-done((bf16[256,768]{1,0:T(8,128)(2,1)S(1)}, bf16[256,768]{1,0:T(8,128)(2,1)}, u32[]{:S(2)}) %copy-start.1) | copy-done | bytes 393240
  80.6 0.0 copy-start.2
  80.6 1.0 %copy-done.2 = bf16[256,768]{1,0:T(8,128)(2,1)S(1)} copy-done((bf16[256,768]{1,0:T(8,128)(2,1)S(1)}, bf16[256,768]{1,0:T(8,128)(2,1)}, u32[]{:S(2)}) %copy-start.2) | copy-done | bytes 393240
  81.6 0.0 copy-start.3
  81.6 1.0 %copy-done.3 = bf16[256,768]{1,0:T(8,128)(2,1)S(1)} copy-done((bf16[256,768]{1,0:T(8,128)(2,1)S(1)}, bf16[256,768]{1,0:T(8,128)(2,1)}, u32[]{:S(2)}) %copy-start.3) | copy-done | bytes 393240
  82.6 8.2 %weight_grads.1 = (bf16[1,768,4096]{2,1,0:T(8,128)(2,1)}, bf16[1,768,4096]{2,1,0:T(8,128)(2,1)}, bf16[1,768,4096]{2,1,0:T(8,128)(2,1)}) custom-call(bf16[256,4096]{1,0:T(8,128)(2,1)S(1)} %copy-done, bf16[256,768]{1,0:T(8,128)(2,1)S(1)} %copy-done.1, bf16[256,768]{1,0:T(8,128)(2,1)S(1)} %copy-done.2, bf16[256,768]{1,0:T(8,128)(2,1)S(1)} %copy-done.3), custom_call_target="tpu_custom_call" | custom-call | tf_op jit(solution)/shard_map/weight_grads/pallas_call | solution.py:409
Async XLA Ops:
  3.5 73.8 %copy-start.4 = (s32[4,8]{1,0:T(4,128)S(1)}, s32[4,8]{1,0:T(4,128)}, u32[]{:S(2)}) copy-start(s32[4,8]{1,0:T(4,128)} %param.9) | copy-start | bytes 388
  78.0 1.6 %copy-start = (bf16[256,4096]{1,0:T(8,128)(2,1)S(1)}, bf16[256,4096]{1,0:T(8,128)(2,1)}, u32[]{:S(2)}) copy-start(bf16[256,4096]{1,0:T(8,128)(2,1)} %get-tuple-element.17.z_ref) | copy-start | bytes 6291460
  79.6 1.0 %copy-start.1 = (bf16[256,768]{1,0:T(8,128)(2,1)S(1)}, bf16[256,768]{1,0:T(8,128)(2,1)}, u32[]{:S(2)}) copy-start(bf16[256,768]{1,0:T(8,128)(2,1)} %get-tuple-element.18.low_ref) | copy-start | bytes 1179652
  80.6 1.0 %copy-start.2 = (bf16[256,768]{1,0:T(8,128)(2,1)S(1)}, bf16[256,768]{1,0:T(8,128)(2,1)}, u32[]{:S(2)}) copy-start(bf16[256,768]{1,0:T(8,128)(2,1)} %get-tuple-element.19.upper_ref) | copy-start | bytes 1179652
  81.6 1.0 %copy-start.3 = (bf16[256,768]{1,0:T(8,128)(2,1)S(1)}, bf16[256,768]{1,0:T(8,128)(2,1)}, u32[]{:S(2)}) copy-start(bf16[256,768]{1,0:T(8,128)(2,1)} %get-tuple-element.20.hid_ref) | copy-start | bytes 1179652

commit v3 on v2

--- a/solution.py
+++ b/solution.py
@@ -11,6 +11,7 @@
 LANES = 128
 UNIT = 8
 CHUNKS = 4
+PULLS = 4
 VMEM_BYTES = 62 * 1024 * 1024
 
 
@@ -124,22 +125,26 @@
 
 def add_to(dst, terms, lead):
     total = 1
-    for n in lead:
+    for n in lead[:-1]:
         total *= n
 
     def step(i, carry):
         index, rest = [], i
-        for n in reversed(lead):
+        for n in reversed(lead[:-1]):
             index.insert(0, rest % n)
             rest = rest // n
-        at = tuple(index) + (slice(None), slice(None))
-        acc = dst[at].astype(jnp.float32)
-        for term in terms:
-            acc = acc + term[at].astype(jnp.float32)
-        dst[at] = acc.astype(dst.dtype)
+        for last in range(lead[-1]):
+            at = tuple(index) + (last, slice(None), slice(None))
+            acc = dst[at].astype(jnp.float32)
+            for term in terms:
+                acc = acc + term[at].astype(jnp.float32)
+            dst[at] = acc.astype(dst.dtype)
         return carry
 
-    lax.fori_loop(0, total, step, 0)
+    if total == 1:
+        step(0, 0)
+    else:
+        lax.fori_loop(0, total, step, 0)
 
 
 def scatter_steps(p, sender, every, buf, landing, out, cols, u_first):
@@ -211,14 +216,14 @@
 
 
 def layer_kernel(groups, hi, *refs):
-    x_ref, m_ref, gate_hbm, up_hbm, down_hbm = refs[0:5]
-    out_ref, inner_ref, z_ref, low_ref, upper_ref, hid_ref = refs[5:11]
-    gate_w, up_w, down_w, buf, mbuf, inner_s = refs[11:17]
-    landing = [refs[17 + 4 * c : 21 + 4 * c] for c in range(CHUNKS + 1)]
-    send_sem, recv_sem, local = refs[21 + 4 * CHUNKS :]
+    tok_ref, dy_ref, m_ref, gate_hbm, up_hbm, down_hbm = refs[0:6]
+    out_ref, inner_ref, z_ref, low_ref, upper_ref, hid_ref = refs[6:12]
+    gate_w, up_w, down_w, buf, mbuf, inner_s, x_ref = refs[12:19]
+    landing = [refs[19 + 4 * c : 23 + 4 * c] for c in range(CHUNKS + 1)]
+    send_sem, recv_sem, local = refs[23 + 4 * CHUNKS :]
     p = Place(groups, hi)
     d, z, u, v = p.d, p.z, p.u, p.v
-    width = x_ref.shape[1]
+    width = tok_ref.shape[1]
     hidden_dim = gate_w.shape[0]
     rows = z_ref.shape[0]
     loads = []
@@ -226,6 +231,8 @@
         copy = pltpu.make_async_copy(src, dst, local.at[i])
         copy.start()
         loads.append(copy)
+    both = [ref[...].astype(jnp.float32) for ref in (tok_ref, dy_ref)]
+    x_ref[...] = jnp.concatenate(both, axis=0).astype(jnp.bfloat16)
     own = []
     for i, (src, dst) in enumerate(((x_ref, buf), (m_ref, mbuf))):
         copy = pltpu.make_async_copy(src, dst.at[v, u, d, z], local.at[3 + i])
@@ -235,7 +242,10 @@
     sender = Sender(send_sem, recv_sem)
     span = width // CHUNKS
     cuts = [(slice(c * span, (c + 1) * span), c % 2 == 1) for c in range(CHUNKS)]
-    sources = [(x_ref, buf, cols, order) for cols, order in cuts]
+    pull = width // PULLS
+    sources = [
+        (x_ref, buf, slice(c * pull, (c + 1) * pull), c % 2 == 1) for c in range(PULLS)
+    ]
     sources.append((m_ref, mbuf, slice(0, LANES), False))
     moves = gather(p, sender, sources)
     next(moves)
@@ -331,13 +341,13 @@
             fresh = scatter_steps(p, sender, every, buf, landing[t], out_ref, cols, order)
             lines.append(fresh)
             next(fresh)
-        for line in lines[: t + 1]:
+        for line in lines[1 : t + 1] + lines[:1]:
             next(line, None)
     for copy in every:
         copy.wait_send()
 
 
-def layer(groups, hi, x, m, gate_local, up_local, down_local):
+def layer(groups, hi, x, dy, m, gate_local, up_local, down_local):
     lead = (2, 2, groups, hi)
     rows = 4 * groups * hi * UNIT
     hidden_dim, width = gate_local.shape
@@ -351,7 +361,7 @@
             pltpu.VMEM((hi - 1, UNIT, cols), dtype),
         ]
 
-    moved = CHUNKS + 1
+    moved = max(CHUNKS, PULLS) + 1
     copies = moved * 2 * (hi - 1 + groups - 1 + 1 + 2 * groups + 4)
     vmem = pl.BlockSpec(memory_space=pltpu.VMEM)
     weight = pltpu.VMEM((hidden_dim, width), jnp.bfloat16)
@@ -365,7 +375,7 @@
             half,
             half,
         ],
-        in_specs=[vmem] * 2 + [pl.BlockSpec(memory_space=pl.ANY)] * 3,
+        in_specs=[vmem] * 3 + [pl.BlockSpec(memory_space=pl.ANY)] * 3,
         out_specs=[vmem] * 6,
         scratch_shapes=[weight] * 3
         + [
@@ -373,6 +383,7 @@
             pltpu.VMEM(lead + (UNIT, LANES), jnp.float32),
         ]
         + [pltpu.VMEM((min(rows, 256), LANES), jnp.float32)]
+        + [pltpu.VMEM((UNIT, width), jnp.bfloat16)]
         + sum([landing(width // CHUNKS, jnp.bfloat16, c % 2 == 1) for c in range(CHUNKS)], [])
         + landing(LANES, jnp.float32, True)
         + [
@@ -384,7 +395,7 @@
             collective_id=0, has_side_effects=True, vmem_limit_bytes=VMEM_BYTES
         ),
         name="layer",
-    )(x, m, gate_local, up_local, down_local)
+    )(x, dy, m, gate_local, up_local, down_local)
 
 
 def grad_kernel(z_ref, low_ref, upper_ref, hid_ref, gate_out, up_out, down_out, turned):
@@ -413,7 +424,7 @@
         in_specs=[pl.BlockSpec((rows, tile), lambda n: (0, n)), whole, whole, whole],
         out_specs=[out] * 3,
         scratch_shapes=[pltpu.VMEM((3, hidden_dim, rows), jnp.bfloat16)],
-        compiler_params=pltpu.CompilerParams(vmem_limit_bytes=VMEM_BYTES // 2),
+        compiler_params=pltpu.CompilerParams(vmem_limit_bytes=VMEM_BYTES),
         name="weight_grads",
     )(z_rows, low, upper, hid)
 
@@ -426,10 +437,9 @@
     lanes = jnp.arange(LANES, dtype=jnp.int32)
     chosen = routes[:, :, None] == lanes[None, None, :]
     dense = jnp.sum(jnp.where(chosen, gate_weights[:, :, None], 0.0), axis=1)
-    both = jnp.concatenate([tokens, grad_output], axis=0)
     dense = jnp.concatenate([dense, jnp.zeros_like(dense)], axis=0)
     sums, inner, z_rows, low, upper, hid = layer(
-        groups, hi, both, dense, gate_proj[0], up_proj[0], down_proj[0]
+        groups, hi, tokens, grad_output, dense, gate_proj[0], up_proj[0], down_proj[0]
     )
     grads = weight_grads(z_rows, low, upper, hid)
     inner = inner[:token_count]

time: 91.3 us -> 85.9 us (0.941)
  local copies, waits for them, and re-layouts: 7.43 us -> 2.86 us
  other arithmetic: 2.96 us -> 1.52 us
    unnamed x10 -> x2, local copies, waits for them, and re-layouts: 4.58 us -> 0.01 us
    pallas_call x1, Pallas kernels: 8.22 us -> 10.2 us  [weight_grads(): pl.pallas_call(grad_kernel, grid=(width // tile,), out_shape=[jax.ShapeDt...]
    concatenate x1 -> x0, other arithmetic: 1.44 us -> none  [body(): both = jnp.concatenate([tokens, grad_output], axis=0)]
    pallas_call x1, Pallas kernels: 71.6 us -> 70.2 us  [layer(): pl.pallas_call(functools.partial(layer_kernel, groups, hi), out_shape=[ja...]
where the time goes in v3:
time: 85.9 us; the launch traced here: 85.4 us
  Pallas kernels  80.4 us (94%)
  local copies, waits for them, and re-layouts  2.86 us (3%)
  other arithmetic  1.52 us (2%)
    pallas_call x1, Pallas kernels, layer(): pl.pallas_call(functools.partial(layer_kernel, groups, hi), out_shape=[ja...  70.2 us
    pallas_call x1, Pallas kernels, weight_grads(): pl.pallas_call(grad_kernel, grid=(width // tile,), out_shape=[jax.ShapeDt...  10.2 us

profile of v3, /device:TPU:0, one launch (start us, length us, event | category | flops | bytes accessed | tf_op | source)
XLA Modules:
  0.0 85.4 jit_solution(4955006644491866197)
XLA Ops:
  0.6 0.8 select_reduce_fusion.1
  1.4 0.6 concatenate.3.refs_2_
  2.0 0.0 copy-start
  2.0 70.2 %layer.1 = (bf16[8,4096]{1,0:T(8,128)(2,1)}, f32[8,128]{1,0:T(8,128)}, bf16[256,4096]{1,0:T(8,128)(2,1)}, bf16[256,768]{1,0:T(8,128)(2,1)}, bf16[256,768]{1,0:T(8,128)(2,1)}, /*index=5*/bf16[256,768]{1,0:T(8,128)(2,1)}) custom-call(bf16[4,4096]{1,0:T(4,128)(2,1)} %refs_0_.1, bf16[4,4096]{1,0:T(4,128)(2,1)} %refs_1_.1, f32[8,128]{1,0:T(8,128)} %concatenate.3.refs_2_, ...), custom_call_target="tpu_custom_call" | custom-call | tf_op jit(solution)/shard_map/layer/pallas_call | solution.py:368
  72.2 1.6 %fusion = (bf16[4,4096]{1,0:T(4,128)(2,1)}, bf16[4,4096]{1,0:T(4,128)(2,1)}) fusion(bf16[8,4096]{1,0:T(8,128)(2,1)} %get-tuple-element.15), kind=kLoop, calls=%fused_computation.3 | loop fusion | bytes 131072 | tf_op jit(solution)/shard_map/slice | solution.py:447
  73.8 0.7 slice.11
  74.5 0.0 copy-done
  74.5 0.7 select_reduce_fusion
  75.2 10.2 %weight_grads.1 = (bf16[1,768,4096]{2,1,0:T(8,128)(2,1)}, bf16[1,768,4096]{2,1,0:T(8,128)(2,1)}, bf16[1,768,4096]{2,1,0:T(8,128)(2,1)}) custom-call(bf16[256,4096]{1,0:T(8,128)(2,1)} %get-tuple-element.17.z_ref, bf16[256,768]{1,0:T(8,128)(2,1)} %get-tuple-element.18.low_ref, bf16[256,768]{1,0:T(8,128)(2,1)} %get-tuple-element.19.upper_ref, ...), custom_call_target="tpu_custom_call" | custom-call | tf_op jit(solution)/shard_map/weight_grads/pallas_call | solution.py:420
Async XLA Ops:
  2.0 72.4 %copy-start = (s32[4,8]{1,0:T(4,128)S(1)}, s32[4,8]{1,0:T(4,128)}, u32[]{:S(2)}) copy-start(s32[4,8]{1,0:T(4,128)} %param.9) | copy-start | bytes 388

commit v4 on v3

--- a/solution.py
+++ b/solution.py
@@ -414,7 +414,7 @@
 def weight_grads(z_rows, low, upper, hid):
     rows, width = z_rows.shape
     hidden_dim = low.shape[1]
-    tile = 512
+    tile = 256
     whole = pl.BlockSpec((rows, hidden_dim), lambda n: (0, 0))
     out = pl.BlockSpec((1, hidden_dim, tile), lambda n: (0, 0, n))
     return pl.pallas_call(

time: 85.9 us -> 90.7 us (1.056)
  Pallas kernels: 80.4 us -> 85.1 us
    pallas_call x1, Pallas kernels: 10.2 us -> 14.9 us  [weight_grads(): pl.pallas_call(grad_kernel, grid=(width // tile,), out_shape=[jax.ShapeDt...]
where the time goes in v4:
time: 90.7 us; the launch traced here: 90.1 us
  Pallas kernels  85.1 us (94%)
  local copies, waits for them, and re-layouts  2.86 us (3%)
  other arithmetic  1.52 us (2%)
    pallas_call x1, Pallas kernels, layer(): pl.pallas_call(functools.partial(layer_kernel, groups, hi), out_shape=[ja...  70.2 us
    pallas_call x1, Pallas kernels, weight_grads(): pl.pallas_call(grad_kernel, grid=(width // tile,), out_shape=[jax.ShapeDt...  14.9 us

profile of v4, /device:TPU:0, one launch (start us, length us, event | category | flops | bytes accessed | tf_op | source)
XLA Modules:
  0.0 90.1 jit_solution(14928804489675907185)
XLA Ops:
  0.6 0.8 select_reduce_fusion.1
  1.4 0.6 concatenate.3.refs_2_
  2.0 0.0 copy-start
  2.0 70.2 %layer.1 = (bf16[8,4096]{1,0:T(8,128)(2,1)}, f32[8,128]{1,0:T(8,128)}, bf16[256,4096]{1,0:T(8,128)(2,1)}, bf16[256,768]{1,0:T(8,128)(2,1)}, bf16[256,768]{1,0:T(8,128)(2,1)}, /*index=5*/bf16[256,768]{1,0:T(8,128)(2,1)}) custom-call(bf16[4,4096]{1,0:T(4,128)(2,1)} %refs_0_.1, bf16[4,4096]{1,0:T(4,128)(2,1)} %refs_1_.1, f32[8,128]{1,0:T(8,128)} %concatenate.3.refs_2_, ...), custom_call_target="tpu_custom_call" | custom-call | tf_op jit(solution)/shard_map/layer/pallas_call | solution.py:368
  72.2 1.6 %fusion = (bf16[4,4096]{1,0:T(4,128)(2,1)}, bf16[4,4096]{1,0:T(4,128)(2,1)}) fusion(bf16[8,4096]{1,0:T(8,128)(2,1)} %get-tuple-element.15), kind=kLoop, calls=%fused_computation.3 | loop fusion | bytes 131072 | tf_op jit(solution)/shard_map/slice | solution.py:447
  73.8 0.7 slice.11
  74.5 0.0 copy-done
  74.5 0.7 select_reduce_fusion
  75.2 14.9 %weight_grads.1 = (bf16[1,768,4096]{2,1,0:T(8,128)(2,1)}, bf16[1,768,4096]{2,1,0:T(8,128)(2,1)}, bf16[1,768,4096]{2,1,0:T(8,128)(2,1)}) custom-call(bf16[256,4096]{1,0:T(8,128)(2,1)} %get-tuple-element.17.z_ref, bf16[256,768]{1,0:T(8,128)(2,1)} %get-tuple-element.18.low_ref, bf16[256,768]{1,0:T(8,128)(2,1)} %get-tuple-element.19.upper_ref, ...), custom_call_target="tpu_custom_call" | custom-call | tf_op jit(solution)/shard_map/weight_grads/pallas_call | solution.py:420
Async XLA Ops:
  2.0 72.4 %copy-start = (s32[4,8]{1,0:T(4,128)S(1)}, s32[4,8]{1,0:T(4,128)}, u32[]{:S(2)}) copy-start(s32[4,8]{1,0:T(4,128)} %param.9) | copy-start | bytes 388
